TPU v7x, 32 devices: a whole 2x2x4 slice. The times are simulated.
32 devices in a mesh: band: 8 (over z, y), mp: 4 (over x, core).
Axes of the slice: x: 2, y: 2, z: 4, core: 2. Of those that a mesh axis runs over, the one named last changes fastest.
Arguments:
- cells: bfloat16 [2048, 1024], P('band', 'mp'), may hold values from -81 to 81
- row_gain: float32 [1024], replicated, may hold values from 0.1 to 1.9
- row_qkv: bfloat16 [3, 1024, 1024], P(None, None, 'mp'), may hold values from -1.25 to 1.25
- row_out: bfloat16 [1024, 1024], P('mp'), may hold values from -0.1875 to 0.1875
- col_gain: float32 [1024], replicated, may hold values from 0.1 to 1.9
- col_qkv: bfloat16 [3, 1024, 1024], P(None, None, 'mp'), may hold values from -1.25 to 1.25
- col_out: bfloat16 [1024, 1024], P('mp'), may hold values from -0.1875 to 0.1875
- row_seg: int32 [2048], P('band'), may hold values from 0 to 255, never falling along the last dimension, each value on 1 to 16 neighbouring positions
- col_dest: int32 [2048, 1], P('band'), may hold values from 0 to 7; in each aligned block of 256 rows (0 to 255, 256 to 511, ...) at most 48 rows name the same one
- sheet_column_index: int32 [2048], P('band'), may hold values from 1 to 8
- d_result: bfloat16 [2048, 1024], P('band', 'mp'), may hold values from -6 to 6
Outputs:
- result: bfloat16 [2048, 1024], P('band', 'mp')
- d_cells: bfloat16 [2048, 1024], P('band', 'mp')
Inputs may be any that keep to these rules, and one draw needn't show every extreme that they name: `row_seg`: cells never fall in value along the array. `col_dest`: at most 48 of the cells of one row band name the same column band, and some row band sends exactly 48 to some column band.
All inputs are finite; a program needn't handle non-finite values.
Results may differ from a plain program's by a relative error of at most 0.019.
Values may be sent and summed in bfloat16 or wider, within the bound.
A program may use at most 64 MiB of HBM per device.

v0:
```python
import jax
import jax.numpy as jnp
from jax import lax
from jax.sharding import PartitionSpec as P

HEAD_DIM = 64
TILE = 128
norm_eps = 1e-06
neg_fill = -1e30


def block_terms(inputs, norm_gain, query_key_value_weight, w_out, allowed, tile_rows):
    values = inputs.astype(jnp.float32)
    inv_rms = lax.rsqrt(jnp.mean(values * values, axis=-1, keepdims=True) + norm_eps)
    normalized_cells = (values * inv_rms * norm_gain).astype(jnp.bfloat16)
    projected_heads = jnp.einsum(
        "lu,xuh->xlh", normalized_cells, query_key_value_weight, preferred_element_type=jnp.float32
    ).astype(jnp.bfloat16)
    row_count = inputs.shape[0]
    feat_width = query_key_value_weight.shape[2]
    head_count = feat_width // HEAD_DIM
    shaped = projected_heads.reshape(3, row_count // tile_rows, tile_rows, head_count, HEAD_DIM)
    scores = jnp.einsum(
        "bqhe,bkhe->bhqk", shaped[0], shaped[1], preferred_element_type=jnp.float32
    ) * HEAD_DIM ** (-0.5)
    scores = jnp.where(allowed[:, None], scores, neg_fill)
    scores = scores - lax.stop_gradient(jnp.max(scores, axis=-1, keepdims=True))
    expd = jnp.exp(scores)
    attn_probs = (expd / jnp.sum(expd, axis=-1, keepdims=True)).astype(jnp.bfloat16)
    attended = jnp.einsum(
        "bhqk,bkhe->bqhe", attn_probs, shaped[2], preferred_element_type=jnp.float32
    ).astype(jnp.bfloat16)
    attended = attended.reshape(row_count, feat_width)
    return jnp.dot(attended, w_out, preferred_element_type=jnp.float32)


def column_band_mask(col_keys):
    positions = jnp.arange(col_keys.shape[0])
    same_col = (col_keys[:, None] == col_keys[None, :]) & (col_keys[None, :] > 0)
    return (same_col | (positions[:, None] == positions[None, :]))[None]


def widen(block):
    return lax.all_gather(block, "mp", axis=1, tiled=True)


def narrow(terms):
    return lax.psum_scatter(
        terms.astype(jnp.bfloat16), "mp", scatter_dimension=1, tiled=True
    ).astype(jnp.float32)


def move_rows(rows):
    return lax.all_to_all(rows, "band", split_axis=0, concat_axis=0, tiled=True)


def on_device(
    cells,
    row_gain,
    row_qkv,
    row_out,
    col_gain,
    col_qkv,
    col_out,
    row_seg,
    col_dest,
    sheet_column_index,
    d_result,
):
    cell_rows, feat_width = cells.shape
    band_count = lax.axis_size("band")
    capacity = max(2, 3 * cell_rows // (2 * band_count))
    slot_total = band_count * capacity
    gathered = widen(cells)
    row_groups = row_seg.reshape(cell_rows // TILE, TILE)
    row_mask = row_groups[:, :, None] == row_groups[:, None, :]

    def row_local(inputs):
        return block_terms(inputs, row_gain, row_qkv, row_out, row_mask, TILE)

    row_terms, row_pull = jax.vjp(row_local, gathered)
    target = col_dest[:, 0]
    onehot = (target[:, None] == jnp.arange(band_count, dtype=jnp.int32)[None, :]).astype(jnp.int32)
    ranking = jnp.sum((jnp.cumsum(onehot, axis=0) - onehot) * onehot, axis=1)
    slot_index = target * capacity + ranking
    keys_out = (
        jnp.zeros((slot_total,), jnp.bfloat16)
        .at[slot_index]
        .set(sheet_column_index.astype(jnp.bfloat16))
    )
    back_in = jnp.zeros((slot_total, feat_width), jnp.bfloat16).at[slot_index].set(d_result)
    mixed_rows = (cells.astype(jnp.float32) + narrow(row_terms)).astype(jnp.bfloat16)
    outgoing = jnp.zeros((slot_total, feat_width), jnp.bfloat16).at[slot_index].set(mixed_rows)
    arrived, col_keys = (
        lax.all_to_all(outgoing, "band", split_axis=0, concat_axis=0, tiled=True),
        lax.all_to_all(keys_out, "band", split_axis=0, concat_axis=0, tiled=True),
    )
    column_full = widen(arrived)
    col_allowed = column_band_mask(col_keys)

    def col_local(inputs):
        return block_terms(inputs, col_gain, col_qkv, col_out, col_allowed, inputs.shape[0])

    col_terms, col_pull = jax.vjp(col_local, column_full)
    settled = (arrived.astype(jnp.float32) + narrow(col_terms)).astype(jnp.bfloat16)
    result = move_rows(settled)[slot_index]
    d_column = move_rows(back_in)
    (d_col_part,) = col_pull(widen(d_column).astype(jnp.float32))
    d_mixed_col = (d_column.astype(jnp.float32) + narrow(d_col_part.astype(jnp.float32))).astype(
        jnp.bfloat16
    )
    d_mixed = move_rows(d_mixed_col)[slot_index]
    (d_row_part,) = row_pull(widen(d_mixed).astype(jnp.float32))
    d_cells = (d_mixed.astype(jnp.float32) + narrow(d_row_part.astype(jnp.float32))).astype(
        jnp.bfloat16
    )
    return (result, d_cells)


def solution(mesh):
    in_specs = (
        P("band", "mp"),
        P(),
        P(None, None, "mp"),
        P("mp", None),
        P(),
        P(None, None, "mp"),
        P("mp", None),
        P("band"),
        P("band", None),
        P("band"),
        P("band", "mp"),
    )
    out_specs = (P("band", "mp"), P("band", "mp"))
    return jax.shard_map(
        on_device, mesh=mesh, in_specs=in_specs, out_specs=out_specs, check_vma=False
    )
```

profile of v0, /device:TPU:0, one launch (start us, length us, event | category | flops | bytes accessed | tf_op | source)
XLA Modules:
  0.0 187.3 jit_solution(5068009255196758206)
XLA Ops:
  7.2 9.0 %all_gather.12 = bf16[256,1024]{1,0:T(8,128)(2,1)S(1)} all-gather(bf16[256,256]{1,0:T(8,128)(2,1)} %param.11), channel_id=1, replica_groups=mesh['band'=8,'mp'=4] {'mp'}, dimensions={1}, use_global_device_ids=true | all-gather | bytes 655360 | tf_op jit(solution)/shard_map/all_gather | solution.py:44
  24.4 2.2 %scatter_custom_fusion.1 = bf16[384]{0:T(512)(128)(2,1)S(1)} fusion(s32[256]{0:T(256)S(1)} %bitcast.165, bf16[256]{0:T(256)(128)(2,1)S(1)} %convert_element_type.209, bf16[]{:T(256)} %constant.12.clone.1), kind=kCustom, calls=%fused_computation.125 | custom fusion | bytes 770 | tf_op jit(solution)/shard_map/scatter | solution.py:89
  27.3 5.8 %all-to-all-start.1 = ((bf16[8,48,1]{1,2,0:T(2,128)(2,1)}), bf16[8,48,1]{1,2,0:T(2,128)(2,1)S(1)}, u32[]{:S(2)}, u32[]{:S(2)}) async-start(bf16[8,48,1]{1,2,0:T(2,128)(2,1)} %all_to_all.52), calls=%async_computation.2 | async-start | bytes 8192 | tf_op jit(solution)/shard_map/all_to_all | solution.py:96
  33.1 2.5 %scatter_custom_fusion.2 = bf16[384,256]{1,0:T(8,128)(2,1)} fusion(s32[256]{0:T(256)S(1)} %bitcast.166, bf16[256,256]{1,0:T(8,128)(2,1)} %param.21, bf16[]{:T(256)} %constant.12.clone.1), kind=kCustom, calls=%fused_computation.103 | custom fusion | bytes 197120 | tf_op jit(solution)/shard_map/scatter | solution.py:91
  35.6 4.0 %all-to-all-done.1 = bf16[8,48,1]{1,2,0:T(2,128)(2,1)S(1)} async-done(((bf16[8,48,1]{1,2,0:T(2,128)(2,1)}), bf16[8,48,1]{1,2,0:T(2,128)(2,1)S(1)}, u32[]{:S(2)}, u32[]{:S(2)}) %all-to-all-start.1) | async-done | bytes 800 | tf_op jit(solution)/shard_map/all_to_all | solution.py:96
  39.6 3.4 %all-to-all-start.3 = ((bf16[8,48,256]{2,1,0:T(8,128)(2,1)}), bf16[8,48,256]{2,1,0:T(8,128)(2,1)S(1)}, u32[]{:S(2)}, u32[]{:S(2)}) async-start(bf16[8,48,256]{2,1,0:T(8,128)(2,1)} %bitcast.22), calls=%async_computation.5 | async-start | bytes 393216 | tf_op jit(solution)/shard_map/all_to_all | solution.py:54
  43.9 2.2 %reduce-scatter.5.cloned.1.call-done = bf16[256,256]{1,0:T(8,128)(2,1)} async-done(((bf16[256,1024]{1,0:T(8,128)(2,1)}), bf16[256,256]{1,0:T(8,128)(2,1)}) %reduce-scatter.5.cloned.1.call-update) | async-done | bytes 131088 | tf_op jit(solution)/shard_map/reduce_scatter | solution.py:48
  46.2 2.5 %scatter_custom_fusion = bf16[384,256]{1,0:T(8,128)(2,1)} fusion(s32[256]{0:T(256)S(1)} %bitcast.167, bf16[256,256]{1,0:T(8,128)(2,1)} %reduce-scatter.5.cloned.1.call-done, bf16[256,256]{1,0:T(8,128)(2,1)S(1)} %copy-done.12, bf16[]{:T(256)} %constant.12.clone.1), kind=kCustom, calls=%fused_computation.98 | custom fusion | flops 262144 | bytes 458754 | tf_op jit(solution)/shard_map/scatter | solution.py:93
  48.6 2.1 %all-to-all-done.3 = bf16[8,48,256]{2,1,0:T(8,128)(2,1)S(1)} async-done(((bf16[8,48,256]{2,1,0:T(8,128)(2,1)}), bf16[8,48,256]{2,1,0:T(8,128)(2,1)S(1)}, u32[]{:S(2)}, u32[]{:S(2)}) %all-to-all-start.3) | async-done | bytes 196640 | tf_op jit(solution)/shard_map/all_to_all | solution.py:54
  50.7 3.6 %all-to-all-start = ((bf16[8,48,256]{2,1,0:T(8,128)(2,1)}), bf16[8,48,256]{2,1,0:T(8,128)(2,1)S(1)}, u32[]{:S(2)}, u32[]{:S(2)}) async-start(bf16[8,48,256]{2,1,0:T(8,128)(2,1)} %bitcast.10), calls=%async_computation.1 | async-start | bytes 393216 | tf_op jit(solution)/shard_map/all_to_all | solution.py:95
  54.3 8.0 %all_gather.14 = bf16[384,1024]{1,0:T(8,128)(2,1)S(1)} all-gather(bf16[384,256]{1,0:T(8,128)(2,1)S(1)} %bitcast.146), channel_id=1, replica_groups=mesh['band'=8,'mp'=4] {'mp'}, dimensions={1}, use_global_device_ids=true | all-gather | bytes 983040 | tf_op jit(solution)/shard_map/all_gather | solution.py:44
  62.9 8.9 %all_gather.13 = bf16[384,1024]{1,0:T(8,128)(2,1)S(1)} all-gather(bf16[384,256]{1,0:T(8,128)(2,1)S(1)} %bitcast.145), channel_id=1, replica_groups=mesh['band'=8,'mp'=4] {'mp'}, dimensions={1}, use_global_device_ids=true | all-gather | bytes 983040 | tf_op jit(solution)/shard_map/all_gather | solution.py:44
  74.0 3.5 %fusion.76 = (f32[4,384]{1,0:T(4,128)S(1)}, f32[4,384,384]{1,2,0:T(8,128)}) fusion(pred[384,384]{0,1:T(8,128)(4,1)} %fusion.43, bf16[384,4,64]{0,2,1:T(8,128)(2,1)} %bitcast.159, bf16[384,4,64]{0,2,1:T(8,128)(2,1)} %bitcast.156), kind=kOutput, calls=%fused_computation.135 | convolution fusion | flops 77857152 | bytes 2906112 | tf_op jit(solution)/shard_map/jvp()/sub | solution.py:27
  77.5 3.7 %fusion.7 = (f32[4,384]{1,0:T(4,128)S(1)}, bf16[4,384,384]{1,2,0:T(8,128)(2,1)}, bf16[4,384,384]{1,2,0:T(8,128)(2,1)}) fusion(f32[4,384,384]{1,2,0:T(8,128)} %get-tuple-element.13, f32[4,384]{1,0:T(4,128)S(1)} %multiply_divide_fusion, f32[4,384]{1,0:T(4,128)S(1)} %get-tuple-element.12, bf16[4,64,384]{2,1,0:T(8,128)(2,1)S(1)} %bitcast.150, ...), kind=kOutput, calls=%fused_computation.19 | convolution fusion | flops 79624704 | bytes 5130240 | tf_op jit(solution)/shard_map/transpose(jvp(bhqk,bkhe->bqhe))/dot_general | solution.py:30
  81.2 3.9 %fusion.26 = bf16[1,1,384,4,64]{2,4,3,1,0:T(8,128)(2,1)} fusion(bf16[384,4,64]{0,2,1:T(8,128)(2,1)} %bitcast.160, bf16[4,384,384]{1,2,0:T(8,128)(2,1)} %get-tuple-element.14, f32[4,384]{1,0:T(4,128)S(1)} %neg.13, f32[4,384]{1,0:T(4,128)S(1)} %get-tuple-element.12, pred[384,384]{0,1:T(8,128)(4,1)} %fusion.43, bf16[384,4,64]{0,2,1:T(8,128)(2,1)S(1)} %bitcast.157), kind=kOutput, calls=%fused_computation.61 | convolution fusion | flops 156403584 | bytes 1929216 | tf_op jit(solution)/shard_map/transpose(jvp(bqhe,bkhe->bhqk))/dot_general | solution.py:23
  85.2 3.6 %fusion.27 = bf16[1,1,384,4,64]{2,4,3,1,0:T(8,128)(2,1)} fusion(bf16[384,4,64]{0,2,1:T(8,128)(2,1)S(1)} %bitcast.158, bf16[4,384,384]{1,2,0:T(8,128)(2,1)} %get-tuple-element.14, f32[4,384]{1,0:T(4,128)S(1)} %neg.13, f32[4,384]{1,0:T(4,128)S(1)} %get-tuple-element.12, pred[384,384]{0,1:T(8,128)(4,1)} %fusion.43, bf16[384,4,64]{0,2,1:T(8,128)(2,1)S(1)} %bitcast.161), kind=kOutput, calls=%fused_computation.62 | convolution fusion | flops 156403584 | bytes 1929216 | tf_op jit(solution)/shard_map/transpose(jvp(bqhe,bkhe->bhqk))/dot_general | solution.py:23
  96.1 24.4 %reduce-scatter.9.cloned.1.call-done = bf16[384,256]{1,0:T(8,128)(2,1)} async-done(((bf16[384,1024]{1,0:T(8,128)(2,1)}), bf16[384,256]{1,0:T(8,128)(2,1)}) %reduce-scatter.9.cloned.1.call-update) | async-done | bytes 196624 | tf_op jit(solution)/shard_map/reduce_scatter | solution.py:48
  122.3 5.5 %all-to-all-start.4 = ((bf16[8,48,256]{2,1,0:T(8,128)(2,1)}), bf16[8,48,256]{2,1,0:T(8,128)(2,1)S(1)}, u32[]{:S(2)}, u32[]{:S(2)}) async-start(bf16[8,48,256]{2,1,0:T(8,128)(2,1)} %bitcast.41), calls=%async_computation.7 | async-start | bytes 393216 | tf_op jit(solution)/shard_map/all_to_all | solution.py:54
  130.9 4.8 %all-to-all-done.4 = bf16[8,48,256]{2,1,0:T(8,128)(2,1)S(1)} async-done(((bf16[8,48,256]{2,1,0:T(8,128)(2,1)}), bf16[8,48,256]{2,1,0:T(8,128)(2,1)S(1)}, u32[]{:S(2)}, u32[]{:S(2)}) %all-to-all-start.4) | async-done | bytes 196640 | tf_op jit(solution)/shard_map/all_to_all | solution.py:54
  136.9 6.7 %all-gather = bf16[256,1024]{1,0:T(8,128)(2,1)S(1)} all-gather(bf16[256,256]{1,0:T(8,128)(2,1)S(1)} %gather_fusion.1), channel_id=2, replica_groups=mesh['band'=8,'mp'=4] {'mp'}, dimensions={1}, use_global_device_ids=true | all-gather | bytes 655360 | tf_op jit(solution)/shard_map/all_gather | solution.py:44
  148.2 2.2 %fusion.37 = (f32[256]{0:T(256)S(1)}, f32[256,1024]{1,0:T(8,128)S(1)}) fusion(bf16[256,1024]{1,0:T(8,128)(2,1)S(1)} %all_gather.12, f32[1024]{0:T(1024)S(1)} %copy-done.21, bf16[3,1024,256]{2,1,0:T(8,128)(2,1)} %param.13, bf16[3,256,256]{1,2,0:T(8,128)(2,1)S(1)} %reshape.278), kind=kOutput, calls=%fused_computation.77 | convolution fusion | flops 404225792 | bytes 3544064 | tf_op jit(solution)/shard_map/transpose(jvp(lu,xuh->xlh))/dot_general | solution.py:16
  151.5 3.5 %reduce-scatter.7.cloned.1.call-done = bf16[384,256]{1,0:T(8,128)(2,1)} async-done(((bf16[384,1024]{1,0:T(8,128)(2,1)}), bf16[384,256]{1,0:T(8,128)(2,1)}) %reduce-scatter.7.cloned.1.call-update) | async-done | bytes 196624 | tf_op jit(solution)/shard_map/reduce_scatter | solution.py:48
  155.9 13.3 %all_to_all.58 = bf16[8,48,256]{2,1,0:T(8,128)(2,1)S(1)} all-to-all(bf16[8,48,256]{2,1,0:T(8,128)(2,1)S(1)} %bitcast.149), channel_id=1, replica_groups=mesh['band'=8,'mp'=4] {'band'}, dimensions={0} | all-to-all | bytes 393216 | tf_op jit(solution)/shard_map/all_to_all | solution.py:54
  171.0 8.2 %reduce-scatter.11.cloned.1.call-done = bf16[256,256]{1,0:T(8,128)(2,1)} async-done(((bf16[256,1024]{1,0:T(8,128)(2,1)}), bf16[256,256]{1,0:T(8,128)(2,1)}) %reduce-scatter.11.cloned.1.call-update) | async-done | bytes 131088 | tf_op jit(solution)/shard_map/reduce_scatter | solution.py:48
  (120 shorter events, 35.6 us)
Async XLA Ops:
  7.2 64.8 %copy-start = (bf16[3,1024,256]{2,1,0:T(8,128)(2,1)S(1)}, bf16[3,1024,256]{2,1,0:T(8,128)(2,1)}, u32[]{:S(2)}) copy-start(bf16[3,1024,256]{2,1,0:T(8,128)(2,1)} %param.16) | copy-start | bytes 4718596
  7.2 39.0 %reduce-scatter.5.cloned.1.call-start = ((), (), s32[]{:S(2)}) async-start(), calls=%async_computation.9 | async-start | bytes 655360 | tf_op jit(solution)/shard_map/reduce_scatter | solution.py:48
  19.0 3.3 %copy-start.3 = (bf16[256,1024]{1,0:T(8,128)(2,1)S(1)}, bf16[256,1024]{1,0:T(8,128)(2,1)}, u32[]{:S(2)}) copy-start(bf16[256,1024]{1,0:T(8,128)(2,1)} %param.14) | copy-start | bytes 1572868
  19.6 3.8 %copy-start.19 = (s32[256,1]{0,1:T(1,128)S(1)}, s32[256,1]{0,1:T(1,128)}, u32[]{:S(2)}) copy-start(s32[256,1]{0,1:T(1,128)} %param.19) | copy-start | bytes 3076
  19.6 4.7 %copy-start.23 = (s32[256]{0:T(256)S(1)}, s32[256]{0:T(256)}, u32[]{:S(2)}) copy-start(s32[256]{0:T(256)} %param.20) | copy-start | bytes 3076
  20.9 25.3 %copy-start.12 = (bf16[256,256]{1,0:T(8,128)(2,1)S(1)}, bf16[256,256]{1,0:T(8,128)(2,1)}, u32[]{:S(2)}) copy-start(bf16[256,256]{1,0:T(8,128)(2,1)} %param.11) | copy-start | bytes 393220
  22.2 40.2 %copy-start.1 = (bf16[256,1024]{1,0:T(8,128)(2,1)S(1)}, bf16[256,1024]{1,0:T(8,128)(2,1)}, u32[]{:S(2)}) copy-start(bf16[256,1024]{1,0:T(8,128)(2,1)} %param.17) | copy-start | bytes 1572868
  27.3 12.3 %all-to-all-start.1 = ((bf16[8,48,1]{1,2,0:T(2,128)(2,1)}), bf16[8,48,1]{1,2,0:T(2,128)(2,1)S(1)}, u32[]{:S(2)}, u32[]{:S(2)}) async-start(bf16[8,48,1]{1,2,0:T(2,128)(2,1)} %all_to_all.52), calls=%async_computation.2 | async-start | bytes 8192 | tf_op jit(solution)/shard_map/all_to_all | solution.py:96
  39.6 11.1 %all-to-all-start.3 = ((bf16[8,48,256]{2,1,0:T(8,128)(2,1)}), bf16[8,48,256]{2,1,0:T(8,128)(2,1)S(1)}, u32[]{:S(2)}, u32[]{:S(2)}) async-start(bf16[8,48,256]{2,1,0:T(8,128)(2,1)} %bitcast.22), calls=%async_computation.5 | async-start | bytes 393216 | tf_op jit(solution)/shard_map/all_to_all | solution.py:54
  48.6 23.4 %copy-start.20 = (f32[1024]{0:T(1024)S(1)}, f32[1024]{0:T(1024)}, u32[]{:S(2)}) copy-start(f32[1024]{0:T(1024)} %param.15) | copy-start | bytes 12292
  50.7 12.1 %copy-start.7 = (bf16[8,48,256]{2,1,0:T(8,128)(2,1)}, bf16[8,48,256]{2,1,0:T(8,128)(2,1)S(1)}, u32[]{:S(2)}) copy-start(bf16[8,48,256]{2,1,0:T(8,128)(2,1)S(1)} %all-to-all-done.3) | copy-start | bytes 589828
  50.7 12.1 %all-to-all-start = ((bf16[8,48,256]{2,1,0:T(8,128)(2,1)}), bf16[8,48,256]{2,1,0:T(8,128)(2,1)S(1)}, u32[]{:S(2)}, u32[]{:S(2)}) async-start(bf16[8,48,256]{2,1,0:T(8,128)(2,1)} %bitcast.10), calls=%async_computation.1 | async-start | bytes 393216 | tf_op jit(solution)/shard_map/all_to_all | solution.py:95
  54.3 66.2 %reduce-scatter.9.cloned.1.call-start = ((), (), s32[]{:S(2)}) async-start(), calls=%async_computation.11 | async-start | bytes 983040 | tf_op jit(solution)/shard_map/reduce_scatter | solution.py:48
  62.8 10.3 %copy-start.5 = (bf16[8,48,256]{2,1,0:T(8,128)(2,1)}, bf16[8,48,256]{2,1,0:T(8,128)(2,1)S(1)}, u32[]{:S(2)}) copy-start(bf16[8,48,256]{2,1,0:T(8,128)(2,1)S(1)} %all-to-all-done) | copy-start | bytes 589828
  73.9 7.3 %copy-start.8 = (bf16[1,384,256]{1,2,0:T(8,128)(2,1)}, bf16[1,384,256]{1,2,0:T(8,128)(2,1)S(1)}, u32[]{:S(2)}) copy-start(bf16[1,384,256]{1,2,0:T(8,128)(2,1)S(1)} %get-tuple-element.6) | copy-start | bytes 589828
  77.5 3.7 %copy-start.13 = (bf16[1,384,256]{1,2,0:T(8,128)(2,1)S(1)}, bf16[1,384,256]{1,2,0:T(8,128)(2,1)}, u32[]{:S(2)}) copy-start(bf16[1,384,256]{1,2,0:T(8,128)(2,1)} %get-tuple-element.4) | copy-start | bytes 589828
  81.2 3.9 %copy-start.14 = (bf16[1,384,256]{1,2,0:T(8,128)(2,1)S(1)}, bf16[1,384,256]{1,2,0:T(8,128)(2,1)}, u32[]{:S(2)}) copy-start(bf16[1,384,256]{1,2,0:T(8,128)(2,1)} %get-tuple-element.5) | copy-start | bytes 589828
  94.8 34.8 %copy-start.2 = (bf16[256,1024]{1,0:T(8,128)(2,1)S(1)}, bf16[256,1024]{1,0:T(8,128)(2,1)}, u32[]{:S(2)}) copy-start(bf16[256,1024]{1,0:T(8,128)(2,1)} %param.17) | copy-start | bytes 1572868
  122.3 13.5 %all-to-all-start.4 = ((bf16[8,48,256]{2,1,0:T(8,128)(2,1)}), bf16[8,48,256]{2,1,0:T(8,128)(2,1)S(1)}, u32[]{:S(2)}, u32[]{:S(2)}) async-start(bf16[8,48,256]{2,1,0:T(8,128)(2,1)} %bitcast.41), calls=%async_computation.7 | async-start | bytes 393216 | tf_op jit(solution)/shard_map/all_to_all | solution.py:54
  127.8 27.2 %reduce-scatter.7.cloned.1.call-start = ((), (), s32[]{:S(2)}) async-start(), calls=%async_computation.10 | async-start | bytes 983040 | tf_op jit(solution)/shard_map/reduce_scatter | solution.py:48
  129.5 14.1 %copy-start.4 = (bf16[256,1024]{1,0:T(8,128)(2,1)S(1)}, bf16[256,1024]{1,0:T(8,128)(2,1)}, u32[]{:S(2)}) copy-start(bf16[256,1024]{1,0:T(8,128)(2,1)} %param.14) | copy-start | bytes 1572868
  130.8 13.3 %copy-start.10 = (bf16[2,128,4,64]{1,3,2,0:T(8,128)(2,1)S(1)}, bf16[2,128,4,64]{1,3,2,0:T(8,128)(2,1)}, u32[]{:S(2)}) copy-start(bf16[2,128,4,64]{1,3,2,0:T(8,128)(2,1)} %copy-done.9) | copy-start | bytes 393220
  130.9 48.3 %reduce-scatter.11.cloned.1.call-start = ((), (), s32[]{:S(2)}) async-start(), calls=%async_computation.12 | async-start | bytes 655360 | tf_op jit(solution)/shard_map/reduce_scatter | solution.py:48
  148.2 6.7 %copy-start.6 = (bf16[8,48,256]{2,1,0:T(8,128)(2,1)S(1)}, bf16[8,48,256]{2,1,0:T(8,128)(2,1)}, u32[]{:S(2)}) copy-start(bf16[8,48,256]{2,1,0:T(8,128)(2,1)} %copy-done.5) | copy-start | bytes 589828
  (8 other events, 16.6 us)
Sparse Core Ops, SparseCore 0:
  23.6 22.5 reduce-scatter.4
  96.2 24.2 reduce-scatter.8
  131.2 23.7 reduce-scatter.6
  157.4 21.6 reduce-scatter.10
where the time goes:
time: 188 us; the launch traced here: 187 us
  waiting for transfers between devices  49.2 us (26%)
  blocking collectives  45.9 us (24%)
  matrix products  34.5 us (18%)
  starting transfers between devices  18.5 us (10%)
  between operations  14.3 us (8%)
  local copies, waits for them, and re-layouts  12.5 us (7%)
  other arithmetic  12.5 us (7%)
    reduce_scatter x4, waiting for transfers between devices, narrow(): lax.psum_scatter(terms.astype(jnp.bfloat16), 'mp', scatter_dimension=1, t...  38.2 us
    all_gather x4, blocking collectives, widen(): return lax.all_gather(block, 'mp', axis=1, tiled=True)  32.6 us
    all_to_all x1, blocking collectives, move_rows(): return lax.all_to_all(rows, 'band', split_axis=0, concat_axis=0, tiled=True)  13.3 us
    dot_general x6, matrix products, block_terms(): jnp.einsum('bhqk,bkhe->bqhe', attn_probs, shaped[2], preferred_element_ty...  11.2 us
    all_to_all x2, starting transfers between devices, move_rows(): return lax.all_to_all(rows, 'band', split_axis=0, concat_axis=0, tiled=True)  8.9 us
    dot_general x4, matrix products, block_terms(): jnp.einsum('bqhe,bkhe->bhqk', shaped[0], shaped[1], preferred_element_typ...  8.12 us
    dot_general x4, matrix products, block_terms(): jnp.einsum('lu,xuh->xlh', normalized_cells, query_key_value_weight, prefe...  7.28 us
    all_to_all x2, waiting for transfers between devices, move_rows(): return lax.all_to_all(rows, 'band', split_axis=0, concat_axis=0, tiled=True)  6.91 us
  transfers between devices with their start and end apart: 8, of which 7 were waited for; matrix products, arithmetic and copies ran while one was open for 13% of the time, Pallas kernels for 0%

commit v1 on v0

--- a/solution.py
+++ b/solution.py
@@ -7,6 +7,23 @@
 TILE = 128
 norm_eps = 1e-06
 neg_fill = -1e30
+
+
+def joined_along(blocks, dim):
+    dims = list(blocks.shape[1:])
+    dims[dim] *= blocks.shape[0]
+    return jnp.moveaxis(blocks, 0, dim).reshape(dims)
+
+
+def ring_gather(x, axis, dim):
+    size = lax.axis_size(axis)
+    right = [(i, (i + 1) % size) for i in range(size)]
+    blocks = [x]
+    while len(blocks) < size:
+        blocks.append(lax.ppermute(blocks[-1], axis, right))
+    index = lax.axis_index(axis)
+    blocks = jnp.stack(blocks)[(index - jnp.arange(size)) % size]
+    return joined_along(blocks, dim)
 
 
 def block_terms(inputs, norm_gain, query_key_value_weight, w_out, allowed, tile_rows):
@@ -41,7 +58,7 @@
 
 
 def widen(block):
-    return lax.all_gather(block, "mp", axis=1, tiled=True)
+    return ring_gather(block, "mp", 1)
 
 
 def narrow(terms):

time: 188 us -> 238 us (1.27)
  waiting for transfers between devices: 49.2 us -> 91 us
  blocking collectives: 45.9 us -> 13.3 us
  local copies, waits for them, and re-layouts: 12.5 us -> 35.6 us
  other arithmetic: 12.5 us -> 24.1 us
  matrix products: 34.5 us -> 37.1 us
    ppermute x0 -> x12, waiting for transfers between devices: none -> 36.9 us  [ring_gather(): blocks.append(lax.ppermute(blocks[-1], axis, right))]
    all_gather x4 -> x0, blocking collectives: 32.6 us -> none  [widen(): return lax.all_gather(block, 'mp', axis=1, tiled=True)]
    gather x0 -> x4, local copies, waits for them, and re-layouts: none -> 6.63 us  [ring_gather(): blocks = jnp.stack(blocks)[(index - jnp.arange(size)) % size]]
    another operation x2 -> x6, other arithmetic: 0.62 us -> 6.96 us  [the longest x4 6.33 us: ring_gather(): blocks = jnp.stack(blocks)[(index - jnp.arange(size)) % size]]
    convert_element_type x0 -> x3, local copies, waits for them, and re-layouts: none -> 6.2 us  [block_terms(): values = inputs.astype(jnp.float32)]
    transpose x0 -> x2, local copies, waits for them, and re-layouts: none -> 3.54 us  [joined_along(): return jnp.moveaxis(blocks, 0, dim).reshape(dims)]
    unnamed x48 -> x84, local copies, waits for them, and re-layouts: 0.13 us -> 2.93 us
    dot_general x4, matrix products: 3.18 us -> 5.95 us  [block_terms(): return jnp.dot(attended, w_out, preferred_element_type=jnp.float32)]
  transfers between devices with their start and end apart: 8 -> 20, of which waited for: 7 -> 19; matrix products, arithmetic and copies ran while one was open for 13% -> 17% of each run, Pallas kernels for 0% -> 0%
where the time goes in v1:
time: 238 us; the launch traced here: 236 us
  waiting for transfers between devices  91 us (38%)
  matrix products  37.1 us (16%)
  local copies, waits for them, and re-layouts  35.6 us (15%)
  other arithmetic  24.1 us (10%)
  starting transfers between devices  20.7 us (9%)
  between operations  14.5 us (6%)
  blocking collectives  13.3 us (6%)
    reduce_scatter x4, waiting for transfers between devices, narrow(): lax.psum_scatter(terms.astype(jnp.bfloat16), 'mp', scatter_dimension=1, t...  37.7 us
    ppermute x12, waiting for transfers between devices, ring_gather(): blocks.append(lax.ppermute(blocks[-1], axis, right))  36.9 us
    all_to_all x1, blocking collectives, move_rows(): return lax.all_to_all(rows, 'band', split_axis=0, concat_axis=0, tiled=True)  13.3 us
    dot_general x6, matrix products, block_terms(): jnp.einsum('bhqk,bkhe->bqhe', attn_probs, shaped[2], preferred_element_ty...  11.2 us
    all_to_all x2, waiting for transfers between devices, move_rows(): return lax.all_to_all(rows, 'band', split_axis=0, concat_axis=0, tiled=True)  9.61 us
    all_to_all x2, starting transfers between devices, move_rows(): return lax.all_to_all(rows, 'band', split_axis=0, concat_axis=0, tiled=True)  8.9 us
    dot_general x4, matrix products, block_terms(): jnp.einsum('lu,xuh->xlh', normalized_cells, query_key_value_weight, prefe...  7.64 us
    dot_general x4, matrix products, block_terms(): jnp.einsum('bqhe,bkhe->bhqk', shaped[0], shaped[1], preferred_element_typ...  7.15 us
  transfers between devices with their start and end apart: 20, of which 19 were waited for; matrix products, arithmetic and copies ran while one was open for 17% of the time, Pallas kernels for 0%

profile of v1, /device:TPU:0, one launch (start us, length us, event | category | flops | bytes accessed | tf_op | source)
XLA Modules:
  0.0 236.2 jit_solution(8019089373825200144)
XLA Ops:
  7.7 4.8 %collective-permute-done = bf16[256,256]{1,0:T(8,128)(2,1)S(1)} collective-permute-done((bf16[256,256]{1,0:T(8,128)(2,1)}, bf16[256,256]{1,0:T(8,128)(2,1)S(1)}, u32[]{:S(2)}, u32[]{:S(2)}) %collective-permute-start) | collective-permute-done | bytes 131104 | tf_op jit(solution)/shard_map/ppermute | solution.py:23
  14.1 2.9 %collective-permute-done.1 = bf16[256,256]{1,0:T(8,128)(2,1)S(1)} collective-permute-done((bf16[256,256]{1,0:T(8,128)(2,1)S(1)}, bf16[256,256]{1,0:T(8,128)(2,1)S(1)}, u32[]{:S(2)}, u32[]{:S(2)}) %collective-permute-start.1) | collective-permute-done | bytes 131104 | tf_op jit(solution)/shard_map/ppermute | solution.py:23
  17.0 4.4 %collective-permute-done.2 = bf16[256,256]{1,0:T(8,128)(2,1)S(1)} collective-permute-done((bf16[256,256]{1,0:T(8,128)(2,1)S(1)}, bf16[256,256]{1,0:T(8,128)(2,1)S(1)}, u32[]{:S(2)}, u32[]{:S(2)}) %collective-permute-start.2) | collective-permute-done | bytes 131104 | tf_op jit(solution)/shard_map/ppermute | solution.py:23
  38.1 6.6 %all-to-all-start.1 = ((bf16[8,48,1]{1,2,0:T(2,128)(2,1)}), bf16[8,48,1]{1,2,0:T(2,128)(2,1)S(1)}, u32[]{:S(2)}, u32[]{:S(2)}) async-start(bf16[8,48,1]{1,2,0:T(2,128)(2,1)} %all_to_all.52), calls=%async_computation.2 | async-start | bytes 8192 | tf_op jit(solution)/shard_map/all_to_all | solution.py:113
  47.2 4.0 %all-to-all-done.1 = bf16[8,48,1]{1,2,0:T(2,128)(2,1)S(1)} async-done(((bf16[8,48,1]{1,2,0:T(2,128)(2,1)}), bf16[8,48,1]{1,2,0:T(2,128)(2,1)S(1)}, u32[]{:S(2)}, u32[]{:S(2)}) %all-to-all-start.1) | async-done | bytes 800 | tf_op jit(solution)/shard_map/all_to_all | solution.py:113
  51.2 3.4 %all-to-all-start.3 = ((bf16[8,48,256]{2,1,0:T(8,128)(2,1)}), bf16[8,48,256]{2,1,0:T(8,128)(2,1)S(1)}, u32[]{:S(2)}, u32[]{:S(2)}) async-start(bf16[8,48,256]{2,1,0:T(8,128)(2,1)} %bitcast.34), calls=%async_computation.5 | async-start | bytes 393216 | tf_op jit(solution)/shard_map/all_to_all | solution.py:71
  54.6 3.5 %reduce-scatter.5.cloned.1.call-done = bf16[256,256]{1,0:T(8,128)(2,1)} async-done(((bf16[256,1024]{1,0:T(8,128)(2,1)}), bf16[256,256]{1,0:T(8,128)(2,1)}) %reduce-scatter.5.cloned.1.call-update) | async-done | bytes 131088 | tf_op jit(solution)/shard_map/reduce_scatter | solution.py:65
  62.3 3.8 %all-to-all-start = ((bf16[8,48,256]{2,1,0:T(8,128)(2,1)}), bf16[8,48,256]{2,1,0:T(8,128)(2,1)S(1)}, u32[]{:S(2)}, u32[]{:S(2)}) async-start(bf16[8,48,256]{2,1,0:T(8,128)(2,1)} %bitcast.16), calls=%async_computation.1 | async-start | bytes 393216 | tf_op jit(solution)/shard_map/all_to_all | solution.py:112
  66.3 5.0 %collective-permute-done.6 = bf16[384,256]{1,0:T(8,128)(2,1)S(1)} collective-permute-done((bf16[384,256]{1,0:T(8,128)(2,1)S(1)}, bf16[384,256]{1,0:T(8,128)(2,1)S(1)}, u32[]{:S(2)}, u32[]{:S(2)}) %collective-permute-start.6) | collective-permute-done | bytes 196640 | tf_op jit(solution)/shard_map/ppermute | solution.py:23
  76.4 2.9 %collective-permute-done.3 = bf16[384,256]{1,0:T(8,128)(2,1)} collective-permute-done((bf16[384,256]{1,0:T(8,128)(2,1)S(1)}, bf16[384,256]{1,0:T(8,128)(2,1)}, u32[]{:S(2)}, u32[]{:S(2)}) %collective-permute-start.3) | collective-permute-done | bytes 196640 | tf_op jit(solution)/shard_map/ppermute | solution.py:23
  88.3 3.1 %collective-permute-done.5 = bf16[384,256]{1,0:T(8,128)(2,1)S(1)} collective-permute-done((bf16[384,256]{1,0:T(8,128)(2,1)}, bf16[384,256]{1,0:T(8,128)(2,1)S(1)}, u32[]{:S(2)}, u32[]{:S(2)}) %collective-permute-start.5) | collective-permute-done | bytes 196640 | tf_op jit(solution)/shard_map/ppermute | solution.py:23
  97.5 3.0 %copy.72 = f32[384,4,256]{0,2,1:T(8,128)} copy(f32[384,4,256]{2,0,1:T(8,128)} %convert_bitcast_fusion) | data formatting | bytes 3145728 | tf_op jit(solution)/shard_map/jvp()/convert_element_type | solution.py:30
  100.5 3.0 %copy.73 = f32[384,1024]{1,0:T(8,128)} copy(f32[384,1024]{0,1:T(8,128)} %bitcast.176) | data formatting | bytes 3145728 | tf_op jit(solution)/shard_map/jvp()/convert_element_type | solution.py:30
  106.7 2.9 %fusion.72 = (f32[4,384]{1,0:T(4,128)}, f32[4,384,384]{1,2,0:T(8,128)}) fusion(pred[384,384]{0,1:T(8,128)(4,1)S(1)} %fusion.37, bf16[384,4,64]{0,2,1:T(8,128)(2,1)S(1)} %bitcast.202, bf16[384,4,64]{0,2,1:T(8,128)(2,1)S(1)} %bitcast.199), kind=kOutput, calls=%fused_computation.144 | convolution fusion | flops 77857152 | bytes 2906112 | tf_op jit(solution)/shard_map/jvp()/sub | solution.py:44
  110.4 3.7 %fusion.7 = (f32[4,384]{1,0:T(4,128)S(1)}, bf16[4,384,384]{1,2,0:T(8,128)(2,1)}, bf16[4,384,384]{1,2,0:T(8,128)(2,1)}) fusion(f32[4,384,384]{1,2,0:T(8,128)} %get-tuple-element.13, f32[4,384]{1,0:T(4,128)S(1)} %multiply_divide_fusion, f32[4,384]{1,0:T(4,128)} %get-tuple-element.12, bf16[4,64,384]{2,1,0:T(8,128)(2,1)S(1)} %bitcast.190, ...), kind=kOutput, calls=%fused_computation.19 | convolution fusion | flops 79624704 | bytes 5130240 | tf_op jit(solution)/shard_map/transpose(jvp(bhqk,bkhe->bqhe))/dot_general | solution.py:47
  114.7 3.0 %fusion.23 = bf16[1,1,384,4,64]{2,4,3,1,0:T(8,128)(2,1)S(1)} fusion(bf16[384,4,64]{0,2,1:T(8,128)(2,1)S(1)} %bitcast.203, bf16[4,384,384]{1,2,0:T(8,128)(2,1)} %get-tuple-element.14, f32[4,384]{1,0:T(4,128)} %neg.13, f32[4,384]{1,0:T(4,128)} %get-tuple-element.12, pred[384,384]{0,1:T(8,128)(4,1)S(1)} %fusion.37, bf16[384,4,64]{0,2,1:T(8,128)(2,1)S(1)} %bitcast.200), kind=kOutput, calls=%fused_computation.60 | convolution fusion | flops 156403584 | bytes 1929216 | tf_op jit(solution)/shard_map/transpose(jvp(bqhe,bkhe->bhqk))/dot_general | solution.py:40
  117.7 3.6 %fusion.24 = bf16[1,1,384,4,64]{2,4,3,1,0:T(8,128)(2,1)} fusion(bf16[384,4,64]{0,2,1:T(8,128)(2,1)S(1)} %bitcast.201, bf16[4,384,384]{1,2,0:T(8,128)(2,1)} %get-tuple-element.14, f32[4,384]{1,0:T(4,128)} %neg.13, f32[4,384]{1,0:T(4,128)} %get-tuple-element.12, pred[384,384]{0,1:T(8,128)(4,1)S(1)} %fusion.37, bf16[384,4,64]{0,2,1:T(8,128)(2,1)S(1)} %bitcast.204), kind=kOutput, calls=%fused_computation.61 | convolution fusion | flops 156403584 | bytes 1929216 | tf_op jit(solution)/shard_map/transpose(jvp(bqhe,bkhe->bhqk))/dot_general | solution.py:40
  130.1 24.3 %reduce-scatter.9.cloned.1.call-done = bf16[384,256]{1,0:T(8,128)(2,1)} async-done(((bf16[384,1024]{1,0:T(8,128)(2,1)}), bf16[384,256]{1,0:T(8,128)(2,1)}) %reduce-scatter.9.cloned.1.call-update) | async-done | bytes 196624 | tf_op jit(solution)/shard_map/reduce_scatter | solution.py:65
  156.0 5.5 %all-to-all-start.4 = ((bf16[8,48,256]{2,1,0:T(8,128)(2,1)}), bf16[8,48,256]{2,1,0:T(8,128)(2,1)S(1)}, u32[]{:S(2)}, u32[]{:S(2)}) async-start(bf16[8,48,256]{2,1,0:T(8,128)(2,1)} %bitcast.59), calls=%async_computation.7 | async-start | bytes 393216 | tf_op jit(solution)/shard_map/all_to_all | solution.py:71
  161.6 7.9 %all-to-all-done.4 = bf16[8,48,256]{2,1,0:T(8,128)(2,1)S(1)} async-done(((bf16[8,48,256]{2,1,0:T(8,128)(2,1)}), bf16[8,48,256]{2,1,0:T(8,128)(2,1)S(1)}, u32[]{:S(2)}, u32[]{:S(2)}) %all-to-all-start.4) | async-done | bytes 196640 | tf_op jit(solution)/shard_map/all_to_all | solution.py:71
  170.7 4.4 %collective-permute-done.9 = bf16[256,256]{1,0:T(8,128)(2,1)S(1)} collective-permute-done((bf16[256,256]{1,0:T(8,128)(2,1)S(1)}, bf16[256,256]{1,0:T(8,128)(2,1)S(1)}, u32[]{:S(2)}, u32[]{:S(2)}) %collective-permute-start.9) | collective-permute-done | bytes 131104 | tf_op jit(solution)/shard_map/ppermute | solution.py:23
  181.8 3.1 %collective-permute-done.11 = bf16[256,256]{1,0:T(8,128)(2,1)} collective-permute-done((bf16[256,256]{1,0:T(8,128)(2,1)}, bf16[256,256]{1,0:T(8,128)(2,1)}, u32[]{:S(2)}, u32[]{:S(2)}) %collective-permute-start.11) | collective-permute-done | bytes 131104 | tf_op jit(solution)/shard_map/ppermute | solution.py:23
  204.8 13.3 %all_to_all.58 = bf16[8,48,256]{2,1,0:T(8,128)(2,1)S(1)} all-to-all(bf16[8,48,256]{2,1,0:T(8,128)(2,1)S(1)} %bitcast.189), channel_id=1, replica_groups=mesh['band'=8,'mp'=4] {'band'}, dimensions={0} | all-to-all | bytes 393216 | tf_op jit(solution)/shard_map/all_to_all | solution.py:71
  219.9 8.1 %reduce-scatter.11.cloned.1.call-done = bf16[256,256]{1,0:T(8,128)(2,1)} async-done(((bf16[256,1024]{1,0:T(8,128)(2,1)}), bf16[256,256]{1,0:T(8,128)(2,1)}) %reduce-scatter.11.cloned.1.call-update) | async-done | bytes 131088 | tf_op jit(solution)/shard_map/reduce_scatter | solution.py:65
  (193 shorter events, 91.5 us)
Async XLA Ops:
  7.2 97.0 %copy-start = (bf16[3,1024,256]{2,1,0:T(8,128)(2,1)S(1)}, bf16[3,1024,256]{2,1,0:T(8,128)(2,1)}, u32[]{:S(2)}) copy-start(bf16[3,1024,256]{2,1,0:T(8,128)(2,1)} %param.16) | copy-start | bytes 4718596
  7.2 50.9 %reduce-scatter.5.cloned.1.call-start = ((), (), s32[]{:S(2)}) async-start(), calls=%async_computation.9 | async-start | bytes 655360 | tf_op jit(solution)/shard_map/reduce_scatter | solution.py:65
  7.2 5.3 %collective-permute-start = (bf16[256,256]{1,0:T(8,128)(2,1)}, bf16[256,256]{1,0:T(8,128)(2,1)S(1)}, u32[]{:S(2)}, u32[]{:S(2)}) collective-permute-start(bf16[256,256]{1,0:T(8,128)(2,1)} %param.11), channel_id=1, source_target_pairs={{0,1},{1,2},{2,3},{3,0},{4,5},{5,6},{6,7},{7,4},{8,9},{9,10},{10,1... | collective-permute-start | bytes 393224 | tf_op jit(solution)/shard_map/ppermute | solution.py:23
  12.5 4.4 %collective-permute-start.1 = (bf16[256,256]{1,0:T(8,128)(2,1)S(1)}, bf16[256,256]{1,0:T(8,128)(2,1)S(1)}, u32[]{:S(2)}, u32[]{:S(2)}) collective-permute-start(bf16[256,256]{1,0:T(8,128)(2,1)S(1)} %collective-permute-done), channel_id=1, source_target_pairs={{0,1},{1,2},{2,3},{3,0},{4,5},{5,6},{6,7},{7,4},{8,9},{9,10},{10,1... | collective-permute-start | bytes 393224 | tf_op jit(solution)/shard_map/ppermute | solution.py:23
  16.9 4.4 %collective-permute-start.2 = (bf16[256,256]{1,0:T(8,128)(2,1)S(1)}, bf16[256,256]{1,0:T(8,128)(2,1)S(1)}, u32[]{:S(2)}, u32[]{:S(2)}) collective-permute-start(bf16[256,256]{1,0:T(8,128)(2,1)S(1)} %collective-permute-done.1), channel_id=1, source_target_pairs={{0,1},{1,2},{2,3},{3,0},{4,5},{5,6},{6,7},{7,4},{8,9},{9,10},{10,1... | collective-permute-start | bytes 393224 | tf_op jit(solution)/shard_map/ppermute | solution.py:23
  38.1 13.1 %all-to-all-start.1 = ((bf16[8,48,1]{1,2,0:T(2,128)(2,1)}), bf16[8,48,1]{1,2,0:T(2,128)(2,1)S(1)}, u32[]{:S(2)}, u32[]{:S(2)}) async-start(bf16[8,48,1]{1,2,0:T(2,128)(2,1)} %all_to_all.52), calls=%async_computation.2 | async-start | bytes 8192 | tf_op jit(solution)/shard_map/all_to_all | solution.py:113
  51.2 11.1 %all-to-all-start.3 = ((bf16[8,48,256]{2,1,0:T(8,128)(2,1)}), bf16[8,48,256]{2,1,0:T(8,128)(2,1)S(1)}, u32[]{:S(2)}, u32[]{:S(2)}) async-start(bf16[8,48,256]{2,1,0:T(8,128)(2,1)} %bitcast.34), calls=%async_computation.5 | async-start | bytes 393216 | tf_op jit(solution)/shard_map/all_to_all | solution.py:71
  62.3 11.8 %all-to-all-start = ((bf16[8,48,256]{2,1,0:T(8,128)(2,1)}), bf16[8,48,256]{2,1,0:T(8,128)(2,1)S(1)}, u32[]{:S(2)}, u32[]{:S(2)}) async-start(bf16[8,48,256]{2,1,0:T(8,128)(2,1)} %bitcast.16), calls=%async_computation.1 | async-start | bytes 393216 | tf_op jit(solution)/shard_map/all_to_all | solution.py:112
  66.1 88.3 %reduce-scatter.9.cloned.1.call-start = ((), (), s32[]{:S(2)}) async-start(), calls=%async_computation.11 | async-start | bytes 983040 | tf_op jit(solution)/shard_map/reduce_scatter | solution.py:65
  66.2 5.1 %collective-permute-start.6 = (bf16[384,256]{1,0:T(8,128)(2,1)S(1)}, bf16[384,256]{1,0:T(8,128)(2,1)S(1)}, u32[]{:S(2)}, u32[]{:S(2)}) collective-permute-start(bf16[384,256]{1,0:T(8,128)(2,1)S(1)} %bitcast.184), channel_id=1, source_target_pairs={{0,1},{1,2},{2,3},{3,0},{4,5},{5,6},{6,7},{7,4},{8,9},{9,10},{10,1... | collective-permute-start | bytes 589832 | tf_op jit(solution)/shard_map/ppermute | solution.py:23
  71.3 5.1 %collective-permute-start.7 = (bf16[384,256]{1,0:T(8,128)(2,1)S(1)}, bf16[384,256]{1,0:T(8,128)(2,1)S(1)}, u32[]{:S(2)}, u32[]{:S(2)}) collective-permute-start(bf16[384,256]{1,0:T(8,128)(2,1)S(1)} %collective-permute-done.6), channel_id=1, source_target_pairs={{0,1},{1,2},{2,3},{3,0},{4,5},{5,6},{6,7},{7,4},{8,9},{9,10},{10,1... | collective-permute-start | bytes 589832 | tf_op jit(solution)/shard_map/ppermute | solution.py:23
  74.1 5.2 %collective-permute-start.3 = (bf16[384,256]{1,0:T(8,128)(2,1)S(1)}, bf16[384,256]{1,0:T(8,128)(2,1)}, u32[]{:S(2)}, u32[]{:S(2)}) collective-permute-start(bf16[384,256]{1,0:T(8,128)(2,1)S(1)} %bitcast.182), channel_id=1, source_target_pairs={{0,1},{1,2},{2,3},{3,0},{4,5},{5,6},{6,7},{7,4},{8,9},{9,10},{10,1... | collective-permute-start | bytes 589832 | tf_op jit(solution)/shard_map/ppermute | solution.py:23
  76.4 5.1 %collective-permute-start.8 = (bf16[384,256]{1,0:T(8,128)(2,1)S(1)}, bf16[384,256]{1,0:T(8,128)(2,1)S(1)}, u32[]{:S(2)}, u32[]{:S(2)}) collective-permute-start(bf16[384,256]{1,0:T(8,128)(2,1)S(1)} %collective-permute-done.7), channel_id=1, source_target_pairs={{0,1},{1,2},{2,3},{3,0},{4,5},{5,6},{6,7},{7,4},{8,9},{9,10},{10,1... | collective-permute-start | bytes 589832 | tf_op jit(solution)/shard_map/ppermute | solution.py:23
  79.3 6.6 %collective-permute-start.4 = (bf16[384,256]{1,0:T(8,128)(2,1)}, bf16[384,256]{1,0:T(8,128)(2,1)}, u32[]{:S(2)}, u32[]{:S(2)}) collective-permute-start(bf16[384,256]{1,0:T(8,128)(2,1)} %collective-permute-done.3), channel_id=1, source_target_pairs={{0,1},{1,2},{2,3},{3,0},{4,5},{5,6},{6,7},{7,4},{8,9},{9,10},{10,1... | collective-permute-start | bytes 589832 | tf_op jit(solution)/shard_map/ppermute | solution.py:23
  85.9 5.5 %collective-permute-start.5 = (bf16[384,256]{1,0:T(8,128)(2,1)}, bf16[384,256]{1,0:T(8,128)(2,1)S(1)}, u32[]{:S(2)}, u32[]{:S(2)}) collective-permute-start(bf16[384,256]{1,0:T(8,128)(2,1)} %collective-permute-done.4), channel_id=1, source_target_pairs={{0,1},{1,2},{2,3},{3,0},{4,5},{5,6},{6,7},{7,4},{8,9},{9,10},{10,1... | collective-permute-start | bytes 589832 | tf_op jit(solution)/shard_map/ppermute | solution.py:23
  128.7 32.9 %copy-start.38 = (s32[256,1]{0,1:T(1,128)S(1)}, s32[256,1]{0,1:T(1,128)}, u32[]{:S(2)}) copy-start(s32[256,1]{0,1:T(1,128)} %copy-done.37) | copy-start | bytes 3076
  128.7 42.0 %copy-start.40 = (f32[2,4,128]{2,1,0:T(4,128)S(1)}, f32[2,4,128]{2,1,0:T(4,128)}, u32[]{:S(2)}) copy-start(f32[2,4,128]{2,1,0:T(4,128)} %copy-done.39) | copy-start | bytes 12292
  130.0 50.2 %copy-start.3 = (bf16[256,1024]{1,0:T(8,128)(2,1)S(1)}, bf16[256,1024]{1,0:T(8,128)(2,1)}, u32[]{:S(2)}) copy-start(bf16[256,1024]{1,0:T(8,128)(2,1)} %param.17) | copy-start | bytes 1572868
  156.0 13.5 %all-to-all-start.4 = ((bf16[8,48,256]{2,1,0:T(8,128)(2,1)}), bf16[8,48,256]{2,1,0:T(8,128)(2,1)S(1)}, u32[]{:S(2)}, u32[]{:S(2)}) async-start(bf16[8,48,256]{2,1,0:T(8,128)(2,1)} %bitcast.59), calls=%async_computation.7 | async-start | bytes 393216 | tf_op jit(solution)/shard_map/all_to_all | solution.py:71
  161.5 42.3 %reduce-scatter.7.cloned.1.call-start = ((), (), s32[]{:S(2)}) async-start(), calls=%async_computation.10 | async-start | bytes 983040 | tf_op jit(solution)/shard_map/reduce_scatter | solution.py:65
  170.7 4.4 %collective-permute-start.9 = (bf16[256,256]{1,0:T(8,128)(2,1)S(1)}, bf16[256,256]{1,0:T(8,128)(2,1)S(1)}, u32[]{:S(2)}, u32[]{:S(2)}) collective-permute-start(bf16[256,256]{1,0:T(8,128)(2,1)S(1)} %gather_fusion.4), channel_id=1, source_target_pairs={{0,1},{1,2},{2,3},{3,0},{4,5},{5,6},{6,7},{7,4},{8,9},{9,10},{10,1... | collective-permute-start | bytes 393224 | tf_op jit(solution)/shard_map/ppermute | solution.py:23
  175.7 4.5 %collective-permute-start.10 = (bf16[256,256]{1,0:T(8,128)(2,1)S(1)}, bf16[256,256]{1,0:T(8,128)(2,1)}, u32[]{:S(2)}, u32[]{:S(2)}) collective-permute-start(bf16[256,256]{1,0:T(8,128)(2,1)S(1)} %collective-permute-done.9), channel_id=1, source_target_pairs={{0,1},{1,2},{2,3},{3,0},{4,5},{5,6},{6,7},{7,4},{8,9},{9,10},{10,1... | collective-permute-start | bytes 393224 | tf_op jit(solution)/shard_map/ppermute | solution.py:23
  180.2 4.7 %collective-permute-start.11 = (bf16[256,256]{1,0:T(8,128)(2,1)}, bf16[256,256]{1,0:T(8,128)(2,1)}, u32[]{:S(2)}, u32[]{:S(2)}) collective-permute-start(bf16[256,256]{1,0:T(8,128)(2,1)} %collective-permute-done.10), channel_id=1, source_target_pairs={{0,1},{1,2},{2,3},{3,0},{4,5},{5,6},{6,7},{7,4},{8,9},{9,10},{10,1... | collective-permute-start | bytes 393224 | tf_op jit(solution)/shard_map/ppermute | solution.py:23
  181.6 46.5 %reduce-scatter.11.cloned.1.call-start = ((), (), s32[]{:S(2)}) async-start(), calls=%async_computation.12 | async-start | bytes 655360 | tf_op jit(solution)/shard_map/reduce_scatter | solution.py:65
  (38 other events, 245.9 us)
Sparse Core Ops, SparseCore 0:
  34.3 23.7 reduce-scatter.4
  130.2 24.1 reduce-scatter.8
  181.7 22.1 reduce-scatter.6
  206.3 21.6 reduce-scatter.10
